TPU v7x, 32 devices: a whole 2x2x4 slice. The times are simulated.
32 devices in a mesh: parts: 2 (over y), row: 4 (over x, core), col: 4 (over z).
Axes of the slice: x: 2, y: 2, z: 4, core: 2. Of those that a mesh axis runs over, the one named last changes fastest.
Arguments:
- basis: float32 [2048, 16384], P(('parts', 'row'), 'col'), parts along dimension 0, may hold values from -6 to 6
- panel_one: float32 [32768, 256], P(('parts', 'col', 'row')), parts along dimension 0, may hold values from -192 to 192
- panel_two: float32 [32768, 256], P(('parts', 'col', 'row')), parts along dimension 0, may hold values from -192 to 192
- gradient: float32 [2048, 512], P(('parts', 'row')), parts along dimension 0, may hold values from -0.25 to 0.25
Outputs:
- new_basis: float32 [2048, 16384], P(('parts', 'row'), 'col'), parts along dimension 0
- rotated: float32 [1024, 16384], P(('parts', 'row'), 'col'), parts along dimension 0
There are 2 independent parts, one for each index of `parts`. A program takes and returns all parts, laid end to end along the dimension named above; each array names one. Nothing has to cross between parts.
All inputs are finite; a program needn't handle non-finite values.
Results may differ from a plain program's by a relative error of at most 0.0001.
Values sent between devices are 32-bit elements; how exact they have to be, the bound alone decides.
A program may use at most 64 MiB of HBM per device.

v0:
```python
import functools

import jax
import jax.numpy as jnp
from jax import lax
from jax.experimental import pallas as pl
from jax.experimental.pallas import tpu as pltpu
from jax.sharding import PartitionSpec as P

HIGHEST = lax.Precision.HIGHEST
MESH = pl.DeviceIdType.MESH
F32 = jnp.float32
BF16 = jnp.bfloat16


def dot_full(left, right):
    return jnp.dot(left, right, precision=HIGHEST, preferred_element_type=F32)


def split(value):
    high = value.astype(BF16)
    return high, (value - high.astype(F32)).astype(BF16)


def dot_split(left, right, across=0):
    def one(a, b):
        return lax.dot_general(a, b, (((1,), (across,)), ((), ())), preferred_element_type=F32)

    return one(left[0], right[0]) + (one(left[0], right[1]) + one(left[1], right[0]))


def remote(src, dst, send_sem, recv_sem, **device):
    return pltpu.make_async_remote_copy(
        src_ref=src,
        dst_ref=dst,
        send_sem=send_sem,
        recv_sem=recv_sem,
        device_id=device,
        device_id_type=MESH,
    )


def tri_inverse_pair(first, second):
    size = first.shape[0]
    rows = lax.broadcasted_iota(jnp.int32, (size, size), 0)
    cols = lax.broadcasted_iota(jnp.int32, (size, size), 1)
    eye = rows == cols

    def start(gram):
        return jnp.where(eye, 2.0 / jnp.where(eye, gram, 1.0), 0.0)

    def level(i, carry):
        half_rows = lax.shift_right_logical(rows, i)
        half_cols = lax.shift_right_logical(cols, i)
        pick = (half_cols == half_rows + 1) & ((half_rows & 1) == 0)

        def grow(inverse, gram):
            corner = jnp.where(pick, gram, 0.0)
            return inverse - dot_full(dot_full(inverse, corner), inverse)

        return grow(carry[0], first), grow(carry[1], second)

    return lax.fori_loop(0, size.bit_length() - 1, level, (start(first), start(second)))


def kernel(
    dims,
    basis, one, two, gradient,
    fresh, rotated,
    pg, ph, plo, bh, bl, gts, gtl, tsend, tkeep, trecv, xrecv,
    gm, g1, gz, g2, g3src, g3, gfull, yacc, y2, abuf, usend, urecv, ukeep, u2,
    pxs, pxr, pss, psr, g1sem, g2s, g2r, g3s, g3r, g4s, g4r, g5sem,
    ts, tr, xs, xr, ys, yr, as_, ar, u1sem, u2s, u2r,
):
    rows_n, cols_n, n, k, g, heads = dims
    big_r, big_c = cols_n // n, rows_n
    chips, depth = big_r // 2, big_c
    r, z = lax.axis_index("row"), lax.axis_index("col")
    c, x = lax.rem(r, 2), lax.div(r, 2)
    sib = r + 1 - 2 * c

    def chip(d):
        return lax.rem(x + d, chips) * 2 + c

    def chip_from(d):
        return lax.rem(x + chips - d, chips) * 2 + c

    def layer(d):
        return lax.rem(z + d, depth)

    def layer_from(d):
        return lax.rem(z + depth - d, depth)

    def strip(index, size):
        return pl.ds(pl.multiple_of(index * size, size), size)

    barrier = pltpu.get_barrier_semaphore()
    pl.semaphore_signal(barrier, inc=1, device_id={"row": sib}, device_id_type=MESH)
    for d in range(1, chips):
        pl.semaphore_signal(barrier, inc=1, device_id={"row": chip(d)}, device_id_type=MESH)
    for d in range(1, depth):
        pl.semaphore_signal(barrier, inc=1, device_id={"col": layer(d)}, device_id_type=MESH)
    pl.semaphore_wait(barrier, 1 + (chips - 1) + (depth - 1))

    panels = (one, two)
    nh = n // heads
    sends = []

    def go(copy):
        copy.start()
        sends.append(copy)

    def spot(owner, h, j):
        return pg.at[owner, pl.ds(h * nh, nh), pl.ds(j * k, k)]

    def own(h, j):
        return panels[j].at[pl.ds(h * nh, nh)]

    def send_across(h):
        for j in range(2):
            q = 2 * h + j
            for d in range(1, chips):
                go(remote(own(h, j), spot(r, h, j), pxs.at[d - 1, q], pxr.at[d - 1, q], row=chip(d)))

    ahead = (heads + 1) // 2
    for h in range(ahead):
        send_across(h)

    one_t, two_t = one[...].T, two[...].T
    gm[0, :, :k] = dot_full(one_t, one[...])
    gm[0, :, k:] = dot_full(one_t, two[...])
    gm[1, :, :k] = dot_full(two_t, two[...])
    gm[1, :, k:] = jnp.zeros((k, k), F32)
    gram_one = remote(gm.at[1 - c], g1, g1sem.at[0], g1sem.at[1], row=sib)
    go(gram_one)

    for h in range(heads):
        for j in range(2):
            q = 2 * h + j
            go(remote(own(h, j), spot(r, h, j), pss.at[0, q], psr.at[0, q], row=sib))

    for rr in range(big_r):
        bh[rr], bl[rr] = split(basis[:, rr * n:(rr + 1) * n])
    turned_g = gradient[...].T
    for rr in range(big_r):
        at = pl.ds((rr // 2) * g, g)
        gts[rr % 2, at], gtl[rr % 2, at] = split(turned_g[rr * g:(rr + 1) * g])
    for rr in range(big_r):
        tsend[rr] = dot_split((gts[1 - c], gtl[1 - c]), (bh[rr], bl[rr]))
        go(remote(tsend.at[rr], trecv.at[rr], ts.at[rr], tr.at[rr], row=sib))

    gram_one.wait_recv()
    gz[...] = gm[c] + g1[...]
    zs = k // depth
    for d in range(1, depth):
        go(remote(gz.at[strip(layer(d), zs)], g2.at[d - 1], g2s.at[d - 1], g2r.at[d - 1], col=layer(d)))

    for rr in range(big_r):
        tkeep[rr] = dot_split((gts[c], gtl[c]), (bh[rr], bl[rr]))

    def consume(owner, h, halves):
        at = pl.ds(h * nh, nh)
        for j in range(2):
            ph[owner, at, pl.ds(j * k, k)], plo[owner, at, pl.ds(j * k, k)] = split(halves[j])
        yacc[...] += dot_split(
            (bh[owner, :, at], bl[owner, :, at]), (ph[owner, at, :], plo[owner, at, :])
        )

    yacc[...] = jnp.zeros_like(yacc)
    for h in range(heads):
        at = pl.ds(h * nh, nh)
        consume(r, h, (one[at, :], two[at, :]))

    for d in range(1, depth):
        remote(g2.at[d - 1], g2.at[d - 1], g2s.at[d - 1], g2r.at[d - 1], col=layer(d)).wait_recv()
    total = gz[strip(z, zs), :]
    for d in range(1, depth):
        total = total + g2[d - 1]
    g3src[...] = total
    for d in range(1, chips):
        go(remote(g3src, g3.at[d - 1], g3s.at[d - 1], g3r.at[d - 1], row=chip(d)))
    for h in range(ahead, heads):
        send_across(h)

    def take_sibling(slot, owner, h):
        for j in range(2):
            q = 2 * h + j
            remote(spot(owner, h, j), spot(owner, h, j), pss.at[slot, q], psr.at[slot, q], row=sib).wait_recv()
        at = pl.ds(h * nh, nh)
        consume(owner, h, (pg[owner, at, :k], pg[owner, at, k:]))

    def take_chip(d, h):
        owner = chip_from(d)
        for j in range(2):
            q = 2 * h + j
            remote(spot(owner, h, j), spot(owner, h, j), pxs.at[d - 1, q], pxr.at[d - 1, q], row=chip(d)).wait_recv()
            go(remote(spot(owner, h, j), spot(owner, h, j), pss.at[d, q], psr.at[d, q], row=sib))
        at = pl.ds(h * nh, nh)
        consume(owner, h, (pg[owner, at, :k], pg[owner, at, k:]))

    def take_round(h):
        for d in range(1, chips):
            take_chip(d, h)
        for d in range(1, chips):
            take_sibling(d, chip_from(d) + 1 - 2 * c, h)

    for h in range(heads):
        take_sibling(0, sib, h)

    for d in range(1, chips):
        remote(g3.at[d - 1], g3.at[d - 1], g3s.at[d - 1], g3r.at[d - 1], row=chip(d)).wait_recv()
    total = g3src[...]
    for d in range(1, chips):
        total = total + g3[d - 1]
    gfull[c, strip(z, zs), :] = total
    mine = gfull.at[c, strip(z, zs)]
    for d in range(1, depth):
        go(remote(mine, mine, g4s.at[d - 1], g4r.at[d - 1], col=layer(d)))

    for rr in range(big_r):
        remote(trecv.at[rr], trecv.at[rr], ts.at[rr], tr.at[rr], row=sib).wait_recv()
        tkeep[rr] = tkeep[rr] + trecv[rr]

    for h in range(heads - 1):
        take_round(h)

    for d in range(1, depth):
        theirs = gfull.at[c, strip(layer_from(d), zs)]
        remote(theirs, theirs, g4s.at[d - 1], g4r.at[d - 1], col=layer(d)).wait_recv()
    go(remote(gfull.at[c], gfull.at[c], g5sem.at[0], g5sem.at[1], row=sib))

    for rr in range(big_r):
        for d in range(1, chips):
            to = lax.rem(x + d, chips)
            go(remote(tkeep.at[rr, strip(to, g)], xrecv.at[d - 1, rr], xs.at[d - 1, rr], xr.at[d - 1, rr], row=chip(d)))
    take_round(heads - 1)

    rs = basis.shape[0] // depth
    for d in range(1, depth):
        go(remote(yacc.at[strip(layer(d), rs)], y2.at[d - 1], ys.at[d - 1], yr.at[d - 1], col=layer(d)))
    other = gfull.at[1 - c]
    remote(other, other, g5sem.at[0], g5sem.at[1], row=sib).wait_recv()
    factor_one, factor_two = tri_inverse_pair(gfull[0, :, :k], gfull[1, :, :k])
    total = yacc[strip(z, rs), :]
    for d in range(1, depth):
        remote(y2.at[d - 1], y2.at[d - 1], ys.at[d - 1], yr.at[d - 1], col=layer(d)).wait_recv()
        total = total + y2[d - 1]
    weight_one = dot_full(total[:, :k], factor_one)
    weight_two = dot_full(total[:, k:] - dot_full(weight_one, gfull[0, :, k:]), factor_two)
    abuf[strip(z, rs), :k] = weight_one
    abuf[strip(z, rs), k:] = weight_two
    mine = abuf.at[strip(z, rs)]
    for d in range(1, depth):
        go(remote(mine, mine, as_.at[d - 1], ar.at[d - 1], col=layer(d)))
    for d in range(1, depth):
        theirs = abuf.at[strip(layer_from(d), rs)]
        remote(theirs, theirs, as_.at[d - 1], ar.at[d - 1], col=layer(d)).wait_recv()

    weight = split(abuf[...])
    usend[...] = dot_split((gts[1 - c], gtl[1 - c]), weight)
    turn = remote(usend, urecv, u1sem.at[0], u1sem.at[1], row=sib)
    go(turn)
    ukeep[...] = dot_split((gts[c], gtl[c]), weight)

    def update(rr):
        at = slice(rr * n, (rr + 1) * n)
        fresh[:, at] = basis[:, at] - dot_split(weight, (ph[rr], plo[rr]), 1)

    update(0)
    turn.wait_recv()
    ukeep[...] = ukeep[...] + urecv[...]
    for d in range(1, chips):
        to = lax.rem(x + d, chips)
        go(remote(ukeep.at[strip(to, g)], u2.at[d - 1], u2s.at[d - 1], u2r.at[d - 1], row=chip(d)))
    for rr in range(1, big_r):
        update(rr)
    turned = ukeep[strip(x, g), :]
    for d in range(1, chips):
        remote(u2.at[d - 1], u2.at[d - 1], u2s.at[d - 1], u2r.at[d - 1], row=chip(d)).wait_recv()
        turned = turned + u2[d - 1]
    turned = split(turned)
    for rr in range(big_r):
        value = tkeep[rr, strip(x, g), :] - dot_split(turned, (ph[rr], plo[rr]), 1)
        for d in range(1, chips):
            remote(xrecv.at[d - 1, rr], xrecv.at[d - 1, rr], xs.at[d - 1, rr], xr.at[d - 1, rr], row=chip(d)).wait_recv()
            value = value + xrecv[d - 1, rr]
        rotated[:, rr * n:(rr + 1) * n] = value
    for copy in sends:
        copy.wait_send()


def solution(mesh):
    big_r, depth = mesh.shape["row"], mesh.shape["col"]
    chips = big_r // 2

    def shards(basis, one, two, gradient):
        m, cols_n = basis.shape
        n, k = one.shape
        gc = gradient.shape[1]
        g = gc // big_r
        heads = 4 if n % 1024 == 0 else 1
        q = 2 * heads
        xo, zo = max(chips - 1, 1), max(depth - 1, 1)
        dma = pltpu.SemaphoreType.DMA
        vmem = pltpu.VMEM
        scratch = [
            vmem((big_r, n, 2 * k), F32),
            vmem((big_r, n, 2 * k), BF16),
            vmem((big_r, n, 2 * k), BF16),
            vmem((big_r, m, n), BF16),
            vmem((big_r, m, n), BF16),
            vmem((2, chips * g, m), BF16),
            vmem((2, chips * g, m), BF16),
            vmem((big_r, chips * g, n), F32),
            vmem((big_r, chips * g, n), F32),
            vmem((big_r, chips * g, n), F32),
            vmem((xo, big_r, g, n), F32),
            vmem((2, k, 2 * k), F32),
            vmem((k, 2 * k), F32),
            vmem((k, 2 * k), F32),
            vmem((zo, k // depth, 2 * k), F32),
            vmem((k // depth, 2 * k), F32),
            vmem((xo, k // depth, 2 * k), F32),
            vmem((2, k, 2 * k), F32),
            vmem((m, 2 * k), F32),
            vmem((zo, m // depth, 2 * k), F32),
            vmem((m, 2 * k), F32),
            vmem((chips * g, 2 * k), F32),
            vmem((chips * g, 2 * k), F32),
            vmem((chips * g, 2 * k), F32),
            vmem((xo, g, 2 * k), F32),
            dma((xo, q)), dma((xo, q)), dma((chips, q)), dma((chips, q)),
            dma((2,)), dma((zo,)), dma((zo,)), dma((xo,)), dma((xo,)),
            dma((zo,)), dma((zo,)), dma((2,)),
            dma((big_r,)), dma((big_r,)), dma((xo, big_r)), dma((xo, big_r)),
            dma((zo,)), dma((zo,)), dma((zo,)), dma((zo,)),
            dma((2,)), dma((xo,)), dma((xo,)),
        ]
        return pl.pallas_call(
            functools.partial(kernel, (depth, cols_n, n, k, g, heads)),
            out_shape=(
                jax.ShapeDtypeStruct((m, cols_n), F32),
                jax.ShapeDtypeStruct((g, cols_n), F32),
            ),
            in_specs=[pl.BlockSpec(memory_space=pltpu.VMEM)] * 4,
            out_specs=(pl.BlockSpec(memory_space=pltpu.VMEM),) * 2,
            scratch_shapes=scratch,
            compiler_params=pltpu.CompilerParams(
                collective_id=0, has_side_effects=True, vmem_limit_bytes=62 * 1024 * 1024
            ),
        )(basis, one, two, gradient)

    return jax.shard_map(
        shards,
        mesh=mesh,
        in_specs=(
            P(("parts", "row"), "col"),
            P(("parts", "col", "row"), None),
            P(("parts", "col", "row"), None),
            P(("parts", "row"), None),
        ),
        out_specs=(P(("parts", "row"), "col"), P(("parts", "row"), "col")),
        check_vma=False,
    )
```

profile of v0, /device:TPU:0, one launch (start us, length us, event | category | flops | bytes accessed | tf_op | source)
XLA Modules:
  0.0 126.0 jit_solution(4786645988749274274)
XLA Ops:
  0.6 119.2 %shard_map.59 = (f32[256,4096]{1,0:T(8,128)}, f32[128,4096]{1,0:T(8,128)}) custom-call(f32[256,4096]{1,0:T(8,128)} %basis.1, f32[1024,256]{1,0:T(8,128)} %one.1, f32[1024,256]{1,0:T(8,128)} %two.1, f32[256,512]{1,0:T(8,128)} %gradient.1), custom_call_target="tpu_custom_call" | custom-call | tf_op jit(solution)/shard_map/pallas_call | solution.py:339
  119.9 0.0 copy-start
  119.9 4.8 %copy.8 = f32[256,4096]{1,0:T(8,128)} copy(f32[256,4096]{1,0:T(8,128)} %get-tuple-element.4) | data formatting | bytes 8388608
  124.7 0.0 copy-done
  124.7 1.3 %copy.9 = f32[128,4096]{1,0:T(8,128)} copy(f32[128,4096]{1,0:T(8,128)S(1)} %copy-done) | data formatting | bytes 4194304
Async XLA Ops:
  119.9 4.8 %copy-start = (f32[128,4096]{1,0:T(8,128)S(1)}, f32[128,4096]{1,0:T(8,128)}, u32[]{:S(2)}) copy-start(f32[128,4096]{1,0:T(8,128)} %get-tuple-element.5) | copy-start | bytes 6291460
where the time goes:
time: 126 us
  Pallas kernels  119 us (94%)
  local copies, waits for them, and re-layouts  6.13 us (5%)
    pallas_call x1, Pallas kernels, shards(): pl.pallas_call(functools.partial(kernel, (depth, cols_n, n, k, g, heads))...  119 us
    unnamed x4, local copies, waits for them, and re-layouts  6.13 us

commit v1 on v0

--- a/solution.py
+++ b/solution.py
@@ -116,15 +116,15 @@
     def own(h, j):
         return panels[j].at[pl.ds(h * nh, nh)]
 
-    def send_across(h):
-        for j in range(2):
-            q = 2 * h + j
-            for d in range(1, chips):
-                go(remote(own(h, j), spot(r, h, j), pxs.at[d - 1, q], pxr.at[d - 1, q], row=chip(d)))
-
-    ahead = (heads + 1) // 2
-    for h in range(ahead):
-        send_across(h)
+    order = [(j, h) for j in range(2) for h in range(heads)]
+
+    def send_across(j, h):
+        q = 2 * h + j
+        for d in range(1, chips):
+            go(remote(own(h, j), spot(r, h, j), pxs.at[d - 1, q], pxr.at[d - 1, q], row=chip(d)))
+
+    for j, h in order[:heads]:
+        send_across(j, h)
 
     one_t, two_t = one[...].T, two[...].T
     gm[0, :, :k] = dot_full(one_t, one[...])
@@ -134,10 +134,9 @@
     gram_one = remote(gm.at[1 - c], g1, g1sem.at[0], g1sem.at[1], row=sib)
     go(gram_one)
 
-    for h in range(heads):
-        for j in range(2):
-            q = 2 * h + j
-            go(remote(own(h, j), spot(r, h, j), pss.at[0, q], psr.at[0, q], row=sib))
+    for j, h in order:
+        q = 2 * h + j
+        go(remote(own(h, j), spot(r, h, j), pss.at[0, q], psr.at[0, q], row=sib))
 
     for rr in range(big_r):
         bh[rr], bl[rr] = split(basis[:, rr * n:(rr + 1) * n])
@@ -158,18 +157,15 @@
     for rr in range(big_r):
         tkeep[rr] = dot_split((gts[c], gtl[c]), (bh[rr], bl[rr]))
 
-    def consume(owner, h, halves):
-        at = pl.ds(h * nh, nh)
-        for j in range(2):
-            ph[owner, at, pl.ds(j * k, k)], plo[owner, at, pl.ds(j * k, k)] = split(halves[j])
-        yacc[...] += dot_split(
-            (bh[owner, :, at], bl[owner, :, at]), (ph[owner, at, :], plo[owner, at, :])
-        )
+    def consume(owner, j, h, half):
+        at, side = pl.ds(h * nh, nh), pl.ds(j * k, k)
+        high, low = split(half)
+        ph[owner, at, side], plo[owner, at, side] = high, low
+        yacc[:, side] += dot_split((bh[owner, :, at], bl[owner, :, at]), (high, low))
 
     yacc[...] = jnp.zeros_like(yacc)
-    for h in range(heads):
-        at = pl.ds(h * nh, nh)
-        consume(r, h, (one[at, :], two[at, :]))
+    for j, h in order:
+        consume(r, j, h, own(h, j)[...])
 
     for d in range(1, depth):
         remote(g2.at[d - 1], g2.at[d - 1], g2s.at[d - 1], g2r.at[d - 1], col=layer(d)).wait_recv()
@@ -179,33 +175,31 @@
     g3src[...] = total
     for d in range(1, chips):
         go(remote(g3src, g3.at[d - 1], g3s.at[d - 1], g3r.at[d - 1], row=chip(d)))
-    for h in range(ahead, heads):
-        send_across(h)
-
-    def take_sibling(slot, owner, h):
-        for j in range(2):
-            q = 2 * h + j
-            remote(spot(owner, h, j), spot(owner, h, j), pss.at[slot, q], psr.at[slot, q], row=sib).wait_recv()
-        at = pl.ds(h * nh, nh)
-        consume(owner, h, (pg[owner, at, :k], pg[owner, at, k:]))
-
-    def take_chip(d, h):
+    for j, h in order[heads:]:
+        send_across(j, h)
+
+    def take_sibling(slot, owner, j, h):
+        q = 2 * h + j
+        here = spot(owner, h, j)
+        remote(here, here, pss.at[slot, q], psr.at[slot, q], row=sib).wait_recv()
+        consume(owner, j, h, here[...])
+
+    def take_chip(d, j, h):
+        q = 2 * h + j
         owner = chip_from(d)
-        for j in range(2):
-            q = 2 * h + j
-            remote(spot(owner, h, j), spot(owner, h, j), pxs.at[d - 1, q], pxr.at[d - 1, q], row=chip(d)).wait_recv()
-            go(remote(spot(owner, h, j), spot(owner, h, j), pss.at[d, q], psr.at[d, q], row=sib))
-        at = pl.ds(h * nh, nh)
-        consume(owner, h, (pg[owner, at, :k], pg[owner, at, k:]))
-
-    def take_round(h):
-        for d in range(1, chips):
-            take_chip(d, h)
-        for d in range(1, chips):
-            take_sibling(d, chip_from(d) + 1 - 2 * c, h)
-
-    for h in range(heads):
-        take_sibling(0, sib, h)
+        here = spot(owner, h, j)
+        remote(here, here, pxs.at[d - 1, q], pxr.at[d - 1, q], row=chip(d)).wait_recv()
+        go(remote(here, here, pss.at[d, q], psr.at[d, q], row=sib))
+        consume(owner, j, h, here[...])
+
+    def take_round(j, h):
+        for d in range(1, chips):
+            take_chip(d, j, h)
+        for d in range(1, chips):
+            take_sibling(d, chip_from(d) + 1 - 2 * c, j, h)
+
+    for j, h in order:
+        take_sibling(0, sib, j, h)
 
     for d in range(1, chips):
         remote(g3.at[d - 1], g3.at[d - 1], g3s.at[d - 1], g3r.at[d - 1], row=chip(d)).wait_recv()
@@ -221,8 +215,35 @@
         remote(trecv.at[rr], trecv.at[rr], ts.at[rr], tr.at[rr], row=sib).wait_recv()
         tkeep[rr] = tkeep[rr] + trecv[rr]
 
-    for h in range(heads - 1):
-        take_round(h)
+    rs = basis.shape[0] // depth
+    sides = (pl.ds(0, k), pl.ds(k, k))
+
+    def image_out(j):
+        for d in range(1, depth):
+            go(remote(
+                yacc.at[strip(layer(d), rs), sides[j]], y2.at[d - 1, :, sides[j]],
+                ys.at[j, d - 1], yr.at[j, d - 1], col=layer(d),
+            ))
+
+    def image_in(j):
+        total = yacc[strip(z, rs), sides[j]]
+        for d in range(1, depth):
+            here = y2.at[d - 1, :, sides[j]]
+            remote(here, here, ys.at[j, d - 1], yr.at[j, d - 1], col=layer(d)).wait_recv()
+            total = total + here[...]
+        return total
+
+    def weight_out(j, value):
+        abuf[strip(z, rs), sides[j]] = value
+        mine = abuf.at[strip(z, rs), sides[j]]
+        for d in range(1, depth):
+            go(remote(mine, mine, as_.at[j, d - 1], ar.at[j, d - 1], col=layer(d)))
+
+    for j, h in order[:heads]:
+        take_round(j, h)
+    image_out(0)
+    for j, h in order[heads:-1]:
+        take_round(j, h)
 
     for d in range(1, depth):
         theirs = gfull.at[c, strip(layer_from(d), zs)]
@@ -233,28 +254,19 @@
         for d in range(1, chips):
             to = lax.rem(x + d, chips)
             go(remote(tkeep.at[rr, strip(to, g)], xrecv.at[d - 1, rr], xs.at[d - 1, rr], xr.at[d - 1, rr], row=chip(d)))
-    take_round(heads - 1)
-
-    rs = basis.shape[0] // depth
-    for d in range(1, depth):
-        go(remote(yacc.at[strip(layer(d), rs)], y2.at[d - 1], ys.at[d - 1], yr.at[d - 1], col=layer(d)))
     other = gfull.at[1 - c]
     remote(other, other, g5sem.at[0], g5sem.at[1], row=sib).wait_recv()
     factor_one, factor_two = tri_inverse_pair(gfull[0, :, :k], gfull[1, :, :k])
-    total = yacc[strip(z, rs), :]
-    for d in range(1, depth):
-        remote(y2.at[d - 1], y2.at[d - 1], ys.at[d - 1], yr.at[d - 1], col=layer(d)).wait_recv()
-        total = total + y2[d - 1]
-    weight_one = dot_full(total[:, :k], factor_one)
-    weight_two = dot_full(total[:, k:] - dot_full(weight_one, gfull[0, :, k:]), factor_two)
-    abuf[strip(z, rs), :k] = weight_one
-    abuf[strip(z, rs), k:] = weight_two
-    mine = abuf.at[strip(z, rs)]
-    for d in range(1, depth):
-        go(remote(mine, mine, as_.at[d - 1], ar.at[d - 1], col=layer(d)))
-    for d in range(1, depth):
-        theirs = abuf.at[strip(layer_from(d), rs)]
-        remote(theirs, theirs, as_.at[d - 1], ar.at[d - 1], col=layer(d)).wait_recv()
+    weight_one = dot_full(image_in(0), factor_one)
+    weight_out(0, weight_one)
+    cross = dot_full(weight_one, gfull[0, :, k:])
+    take_round(*order[-1])
+    image_out(1)
+    weight_out(1, dot_full(image_in(1) - cross, factor_two))
+    for j in range(2):
+        for d in range(1, depth):
+            theirs = abuf.at[strip(layer_from(d), rs), sides[j]]
+            remote(theirs, theirs, as_.at[j, d - 1], ar.at[j, d - 1], col=layer(d)).wait_recv()
 
     weight = split(abuf[...])
     usend[...] = dot_split((gts[1 - c], gtl[1 - c]), weight)
@@ -333,7 +345,7 @@
             dma((2,)), dma((zo,)), dma((zo,)), dma((xo,)), dma((xo,)),
             dma((zo,)), dma((zo,)), dma((2,)),
             dma((big_r,)), dma((big_r,)), dma((xo, big_r)), dma((xo, big_r)),
-            dma((zo,)), dma((zo,)), dma((zo,)), dma((zo,)),
+            dma((2, zo)), dma((2, zo)), dma((2, zo)), dma((2, zo)),
             dma((2,)), dma((xo,)), dma((xo,)),
         ]
         return pl.pallas_call(

time: 126 us -> 126 us (level)
  no operation moved by 1% of the time
where the time goes in v1:
time: 126 us
  Pallas kernels  119 us (94%)
  local copies, waits for them, and re-layouts  6.13 us (5%)
    pallas_call x1, Pallas kernels, shards(): pl.pallas_call(functools.partial(kernel, (depth, cols_n, n, k, g, heads))...  119 us
    unnamed x4, local copies, waits for them, and re-layouts  6.13 us

profile of v1, /device:TPU:0, one launch (start us, length us, event | category | flops | bytes accessed | tf_op | source)
XLA Modules:
  0.0 126.1 jit_solution(9166202718888128346)
XLA Ops:
  0.6 119.4 %shard_map.59 = (f32[256,4096]{1,0:T(8,128)}, f32[128,4096]{1,0:T(8,128)}) custom-call(f32[256,4096]{1,0:T(8,128)} %basis.1, f32[1024,256]{1,0:T(8,128)} %one.1, f32[1024,256]{1,0:T(8,128)} %two.1, f32[256,512]{1,0:T(8,128)} %gradient.1), custom_call_target="tpu_custom_call" | custom-call | tf_op jit(solution)/shard_map/pallas_call | solution.py:351
  120.0 0.0 copy-start
  120.0 4.8 %copy.8 = f32[256,4096]{1,0:T(8,128)} copy(f32[256,4096]{1,0:T(8,128)} %get-tuple-element.4) | data formatting | bytes 8388608
  124.8 0.0 copy-done
  124.8 1.3 %copy.9 = f32[128,4096]{1,0:T(8,128)} copy(f32[128,4096]{1,0:T(8,128)S(1)} %copy-done) | data formatting | bytes 4194304
Async XLA Ops:
  120.0 4.8 %copy-start = (f32[128,4096]{1,0:T(8,128)S(1)}, f32[128,4096]{1,0:T(8,128)}, u32[]{:S(2)}) copy-start(f32[128,4096]{1,0:T(8,128)} %get-tuple-element.5) | copy-start | bytes 6291460
